TPU v7x, 256 devices: a whole 4x4x8 slice. The times are simulated.
256 devices in a mesh: section: 4 (over x), tok: 64 (over y, z, core).
Axes of the slice: x: 4, y: 4, z: 8, core: 2. Of those that a mesh axis runs over, the one named last changes fastest.
Arguments:
- queries: bfloat16 [4, 8192, 5120], P('section', 'tok'), may hold values from -4 to 4
- keys: bfloat16 [4, 8192, 5120], P('section', 'tok'), may hold values from -12 to 12
- values: bfloat16 [4, 8192, 5120], P('section', 'tok'), may hold values from -4 to 4
- cluster_ids: int32 [4, 8192, 2], P('section', 'tok'), may hold values from 0 to 63, as said below
Outputs:
- handed: bfloat16 [4, 8192, 5120], P('section', 'tok')
Inputs may be any that keep to these rules, and one draw needn't show every extreme that they name: `cluster_ids`: each token names two different clusters. Among the 128 tokens of one index of tok no cluster is named more than 8 times; in every section one cluster is named exactly 8 times by the tokens of every index of tok, and one cluster by none of them.
All inputs are finite; a program needn't handle non-finite values.
Results may differ from a plain program's by a relative error of at most 0.0051.
Values may be sent and summed in bfloat16 or wider, within the bound.
A program may use at most 64 MiB of HBM per device.

v0:
```python
import math

import jax
import jax.numpy as jnp
from jax import lax
from jax.sharding import PartitionSpec as P

HD = 128
WIN = 128
BLOCK = 256


def passed_along(value, axis, by):
    peers = lax.axis_size(axis)
    pairs = [(i, i + by) for i in range(peers) if 0 <= i + by < peers]
    return lax.ppermute(value, axis, pairs)


def prefix(value, axis, combine, identity):
    peers, place = (lax.axis_size(axis), lax.axis_index(axis))
    everything = lax.all_gather(value, axis)
    start = jnp.broadcast_to(jnp.asarray(identity, value.dtype), value.shape)

    def turn(k, before):
        reached = k < place
        new = combine(before, everything[k])
        return jnp.where(reached, new, before)

    return lax.fori_loop(0, peers, turn, start)


def shifted(block, axis, distance):
    devices = range(lax.axis_size(axis))
    route = [((i - distance) % len(devices), i) for i in devices]
    return lax.ppermute(block, axis, route)


def softmax_mix(query_blk, key_blk, value_blk, allowed):
    score_scale = 1.0 / math.sqrt(HD)
    scores = (
        jnp.einsum("bqhe,bkhe->bhqk", query_blk, key_blk, preferred_element_type=jnp.float32)
        * score_scale
    )
    scores = jnp.where(allowed[:, None], scores, -1e30)
    highest = jnp.max(scores, axis=-1, keepdims=True)
    weights = jnp.exp(scores - highest)
    weight_sum = jnp.sum(weights, axis=-1)
    mixed = jnp.einsum(
        "bhqk,bkhe->bqhe",
        weights.astype(jnp.bfloat16),
        value_blk,
        preferred_element_type=jnp.float32,
    )
    return mixed / jnp.transpose(weight_sum, (0, 2, 1))[..., None]


def window_mix(query_loc, key_all, value_all, block_base):
    window_len = key_all.shape[0] - query_loc.shape[0]
    blocks = query_loc.shape[0] // window_len
    heads_here = query_loc.shape[1] // HD
    query_blk = query_loc.reshape(blocks, window_len, heads_here, HD)
    key_blk = jnp.concatenate(
        [
            key_all[:-window_len].reshape(blocks, window_len, heads_here, HD),
            key_all[window_len:].reshape(blocks, window_len, heads_here, HD),
        ],
        axis=1,
    )
    value_blk = jnp.concatenate(
        [
            value_all[:-window_len].reshape(blocks, window_len, heads_here, HD),
            value_all[window_len:].reshape(blocks, window_len, heads_here, HD),
        ],
        axis=1,
    )
    rows_at = jnp.arange(window_len, dtype=jnp.int32)[:, None]
    cols_at = jnp.arange(2 * window_len, dtype=jnp.int32)[None, :]
    inside = (cols_at > rows_at) & (cols_at <= rows_at + window_len)
    opening = block_base + jnp.arange(blocks, dtype=jnp.int32) == 0
    allowed = inside[None] & (
        jnp.logical_not(opening)[:, None, None] | (cols_at >= window_len)[None]
    )
    return (
        softmax_mix(query_blk, key_blk, value_blk, allowed)
        .reshape(query_loc.shape)
        .astype(jnp.bfloat16)
    )


def add_counts(earlier, later):
    return earlier + later


def on_device(queries, keys, values, cluster_ids):
    own_query = queries[0]
    own_key = keys[0]
    own_value = values[0]
    cluster_pick = cluster_ids[0]
    tokens = own_query.shape[0]
    half_width = own_query.shape[1] // 2
    route_heads = half_width // HD
    clusters = lax.axis_size("tok")
    capacity = 4 * tokens
    bound_rows = capacity // clusters
    slot_total = clusters * bound_rows
    blocks = capacity // BLOCK
    tails = jnp.stack(
        [own_key[tokens - WIN :, :half_width], own_value[tokens - WIN :, :half_width]]
    )
    before = passed_along(tails, "tok", 1)
    key_all = jnp.concatenate([before[0], own_key[:, :half_width]], axis=0)
    value_all = jnp.concatenate([before[1], own_value[:, :half_width]], axis=0)
    block_base = lax.axis_index("tok") * (tokens // WIN)
    local_out = window_mix(own_query[:, :half_width], key_all, value_all, block_base)
    route_query = own_query[:, half_width:]
    route_key = own_key[:, half_width:]
    route_value = own_value[:, half_width:]
    member = jnp.sum(
        (cluster_pick[:, :, None] == jnp.arange(clusters, dtype=jnp.int32)[None, None, :]).astype(
            jnp.float32
        ),
        axis=1,
    )
    lower = (jnp.arange(tokens)[:, None] >= jnp.arange(tokens)[None, :]).astype(jnp.float32)
    inclusive = jnp.dot(
        lower, member, precision=lax.Precision.HIGHEST, preferred_element_type=jnp.float32
    )
    counts = inclusive[tokens - 1].astype(jnp.int32)
    local_rank = jnp.take_along_axis(inclusive, cluster_pick, axis=1).astype(jnp.int32) - 1
    token_index = jnp.broadcast_to(jnp.arange(tokens, dtype=jnp.int32)[:, None], (tokens, 2))
    slot_token = (
        jnp.full((clusters, bound_rows), tokens, jnp.int32)
        .at[cluster_pick, local_rank]
        .set(token_index)
    )
    slot_live = slot_token < tokens
    safe_token = jnp.minimum(slot_token, tokens - 1)
    live_col = slot_live[:, :, None]
    nothing = jnp.zeros((), jnp.bfloat16)
    send_query = jnp.where(live_col, route_query[safe_token], nothing)
    send_key = jnp.where(live_col, route_key[safe_token], nothing)
    send_value = jnp.where(live_col, route_value[safe_token], nothing)
    slot_at = jnp.arange(bound_rows, dtype=jnp.int32)[None, :]
    earlier = prefix(counts, "tok", add_counts, jnp.zeros_like(counts))
    global_rank = jnp.where(slot_live, earlier[:, None] + slot_at, capacity)
    got_query, got_key, got_value, position = (
        lax.all_to_all(send_query, "tok", split_axis=0, concat_axis=0, tiled=True),
        lax.all_to_all(send_key, "tok", split_axis=0, concat_axis=0, tiled=True),
        lax.all_to_all(send_value, "tok", split_axis=0, concat_axis=0, tiled=True),
        lax.all_to_all(global_rank, "tok", split_axis=0, concat_axis=0, tiled=True),
    )
    source_slot = (
        jnp.full((capacity,), slot_total, jnp.int32)
        .at[position.reshape(-1)]
        .set(jnp.arange(slot_total, dtype=jnp.int32), mode="drop")
    )
    filled = source_slot < slot_total
    safe_slot = jnp.minimum(source_slot, slot_total - 1)

    def arrange(received):
        return received.reshape(slot_total, half_width)[safe_slot].reshape(
            blocks, BLOCK, route_heads, HD
        )

    places = jnp.arange(BLOCK, dtype=jnp.int32)
    causal = places[None, :] <= places[:, None]
    diagonal = places[None, :] == places[:, None]
    allowed = causal[None] & (filled.reshape(blocks, 1, BLOCK) | diagonal[None])
    routed = (
        softmax_mix(arrange(got_query), arrange(got_key), arrange(got_value), allowed)
        .reshape(capacity, half_width)
        .astype(jnp.bfloat16)
    )
    reply_rows = jnp.where(
        (position < capacity)[:, :, None], routed[jnp.minimum(position, capacity - 1)], nothing
    )
    returned_rows = lax.all_to_all(reply_rows, "tok", split_axis=0, concat_axis=0, tiled=True)
    pick_slot = cluster_pick * bound_rows + local_rank
    gathered = returned_rows.reshape(slot_total, half_width)[pick_slot]
    route_out = (gathered[:, 0].astype(jnp.float32) + gathered[:, 1].astype(jnp.float32)).astype(
        jnp.bfloat16
    )
    layer_out = shifted(jnp.concatenate([local_out, route_out], axis=1), "section", 1)
    return layer_out[None]


def solution(mesh):
    return jax.shard_map(
        on_device,
        mesh=mesh,
        in_specs=(
            P("section", "tok", None),
            P("section", "tok", None),
            P("section", "tok", None),
            P("section", "tok", None),
        ),
        out_specs=P("section", "tok", None),
        check_vma=False,
    )
```

profile of v0, /device:TPU:8, one launch (start us, length us, event | category | flops | bytes accessed | tf_op | source)
XLA Modules:
  0.0 470.6 jit_solution(6081887176654235220)
XLA Ops:
  1.9 42.3 %all-gather = s32[64,1,64]{2,1,0:T(1,128)S(1)} all-gather(s32[1,1,64]{2,1,0:T(1,128)S(1)} %bitcast.129), channel_id=1, replica_groups=mesh['section'=4,'tok'=64] {'tok'}, dimensions={0}, use_global_device_ids=true | all-gather | bytes 16640 | tf_op jit(solution)/shard_map/all_gather | solution.py:21
  49.6 11.3 %scatter_fusion = s32[64,8]{0,1:T(8,128)S(1)} fusion(s32[64,8]{0,1:T(8,128)S(1)} %broadcast.282, s32[256]{0:T(256)S(1)} %reshape.443, s32[256]{0:T(256)S(1)} %reshape.445), kind=kCustom, calls=%fused_computation.9 | custom fusion | bytes 5120 | tf_op jit(solution)/shard_map/scatter | solution.py:134
  61.7 7.3 %all-to-all-start = ((s32[64,1,8]{2,1,0:T(1,128)}), s32[64,1,8]{2,1,0:T(1,128)S(1)}, u32[]{:S(2)}, u32[]{:S(2)}) async-start(s32[64,1,8]{2,1,0:T(1,128)} %copy.110), calls=%async_computation | async-start | bytes 65536 | tf_op jit(solution)/shard_map/all_to_all | solution.py:150
  70.2 3.5 gather_fusion.2
  76.8 3.5 gather_fusion.4
  80.3 3.5 gather_fusion
  83.8 5.1 %bitcast_select_fusion.3 = (bf16[64,8,2560]{2,1,0:T(8,128)(2,1)}, bf16[64,8,2560]{2,1,0:T(8,128)(2,1)S(1)}, bf16[64,8,2560]{2,1,0:T(8,128)(2,1)}) fusion(bf16[512,2560]{1,0:T(8,128)(2,1)} %gather_fusion, pred[64,8]{1,0:T(8,128)(4,1)S(1)} %copy.113, bf16[512,2560]{1,0:T(8,128)(2,1)} %gather_fusion.2, bf16[512,2560]{1,0:T(8,128)(2,1)} %gather_fusion.4), kind=kLoop, calls=%fused_computation.33 | loop fusion | flops 3932160 | bytes 15729152 | tf_op jit(solution)/shard_map/jit(_where)/select_n | solution.py:142
  89.0 71.9 %all_to_all.29 = bf16[64,8,2560]{2,1,0:T(8,128)(2,1)} all-to-all(bf16[64,8,2560]{2,1,0:T(8,128)(2,1)} %get-tuple-element.126), channel_id=1, replica_groups=mesh['section'=4,'tok'=64] {'tok'}, dimensions={0} | all-to-all | bytes 5242880 | tf_op jit(solution)/shard_map/all_to_all | solution.py:149
  160.9 68.4 %all_to_all.30 = bf16[64,8,2560]{2,1,0:T(8,128)(2,1)} all-to-all(bf16[64,8,2560]{2,1,0:T(8,128)(2,1)S(1)} %get-tuple-element.127), channel_id=1, replica_groups=mesh['section'=4,'tok'=64] {'tok'}, dimensions={0} | all-to-all | bytes 5242880 | tf_op jit(solution)/shard_map/all_to_all | solution.py:147
  229.3 7.0 %all-to-all-start.3 = ((bf16[64,8,2560]{2,1,0:T(8,128)(2,1)}), bf16[64,8,2560]{2,1,0:T(8,128)(2,1)S(1)}, u32[]{:S(2)}, u32[]{:S(2)}) async-start(bf16[64,8,2560]{2,1,0:T(8,128)(2,1)} %get-tuple-element.128), calls=%async_computation.3 | async-start | bytes 5242880 | tf_op jit(solution)/shard_map/all_to_all | solution.py:148
  243.0 8.3 %gather_fusion.1 = bf16[512,2560]{1,0:T(8,128)(2,1)} fusion(bf16[512,2560]{1,0:T(8,128)(2,1)} %bitcast.109, s32[1024]{0:T(1024)S(1)} %pad_clamp_fusion.2), kind=kCustom, calls=%fused_computation.1 | custom fusion | bytes 5244928 | tf_op jit(solution)/shard_map/gather | solution.py:161
  251.3 8.2 %gather_fusion.3 = bf16[512,2560]{1,0:T(8,128)(2,1)} fusion(bf16[512,2560]{1,0:T(8,128)(2,1)} %bitcast.110, s32[1024]{0:T(1024)S(1)} %pad_clamp_fusion.2), kind=kCustom, calls=%fused_computation.3 | custom fusion | bytes 5244928 | tf_op jit(solution)/shard_map/gather | solution.py:161
  259.4 37.8 %all-to-all-done.3 = bf16[64,8,2560]{2,1,0:T(8,128)(2,1)S(1)} async-done(((bf16[64,8,2560]{2,1,0:T(8,128)(2,1)}), bf16[64,8,2560]{2,1,0:T(8,128)(2,1)S(1)}, u32[]{:S(2)}, u32[]{:S(2)}) %all-to-all-start.3) | async-done | bytes 2621472 | tf_op jit(solution)/shard_map/all_to_all | solution.py:148
  297.3 3.5 gather_fusion.5
  300.8 5.6 %reshape.473 = bf16[2,256,20,128]{3,2,1,0:T(8,128)(2,1)} reshape(bf16[512,2560]{1,0:T(8,128)(2,1)} %gather_fusion.5) | data formatting | bytes 5242880 | tf_op jit(solution)/shard_map/reshape | solution.py:161
  306.4 5.7 %reshape.472 = bf16[2,256,20,128]{3,2,1,0:T(8,128)(2,1)} reshape(bf16[512,2560]{1,0:T(8,128)(2,1)} %gather_fusion.3) | data formatting | bytes 5242880 | tf_op jit(solution)/shard_map/reshape | solution.py:161
  312.0 3.2 reshape.471
  315.3 4.9 %fusion = (f32[2,20,256]{2,1,0:T(8,128)S(1)}, f32[2,20,256,256]{2,3,1,0:T(8,128)S(1)}) fusion(pred[2,256,256]{1,2,0:T(8,128)(4,1)S(1)} %or_and_fusion, bf16[2,256,20,128]{3,2,1,0:T(8,128)(2,1)} %reshape.473, bf16[2,256,20,128]{3,2,1,0:T(8,128)(2,1)} %reshape.472), kind=kOutput, calls=%fused_computation.15 | convolution fusion | flops 678942720 | bytes 15900672 | tf_op jit(solution)/shard_map/bqhe,bkhe->bhqk/dot_general | solution.py:41
  325.7 3.2 copy.136
  331.3 3.5 gather_fusion.6
  334.8 3.5 bitcast_select_fusion
  338.3 7.2 %all-to-all-start.4 = ((bf16[64,8,2560]{2,1,0:T(8,128)(2,1)}), bf16[64,8,2560]{2,1,0:T(8,128)(2,1)S(1)}, u32[]{:S(2)}, u32[]{:S(2)}) async-start(bf16[64,8,2560]{2,1,0:T(8,128)(2,1)} %bitcast_select_fusion), calls=%async_computation.4 | async-start | bytes 5242880 | tf_op jit(solution)/shard_map/all_to_all | solution.py:177
  358.1 61.2 %collective-permute-done = bf16[2,128,2560]{2,1,0:T(8,128)(2,1)} collective-permute-done((bf16[2,128,2560]{2,1,0:T(8,128)(2,1)}, bf16[2,128,2560]{2,1,0:T(8,128)(2,1)}, u32[]{:S(2)}, u32[]{:S(2)}) %collective-permute-start) | collective-permute-done | bytes 1310752 | tf_op jit(solution)/shard_map/ppermute | solution.py:16
  441.7 27.4 %collective-permute-done.1 = bf16[128,5120]{1,0:T(8,128)(2,1)S(1)} collective-permute-done((bf16[128,5120]{1,0:T(8,128)(2,1)S(1)}, bf16[128,5120]{1,0:T(8,128)(2,1)S(1)}, u32[]{:S(2)}, u32[]{:S(2)}) %collective-permute-start.1) | collective-permute-done | bytes 1310752 | tf_op jit(solution)/shard_map/ppermute | solution.py:35
  (148 shorter events, 63.7 us)
Async XLA Ops:
  49.6 19.7 %copy-start.3 = (bf16[1,128,5120]{2,1,0:T(8,128)(2,1)S(1)}, bf16[1,128,5120]{2,1,0:T(8,128)(2,1)}, u32[]{:S(2)}) copy-start(bf16[1,128,5120]{2,1,0:T(8,128)(2,1)} %param.6) | copy-start | bytes 3932164
  61.7 27.3 %all-to-all-start = ((s32[64,1,8]{2,1,0:T(1,128)}), s32[64,1,8]{2,1,0:T(1,128)S(1)}, u32[]{:S(2)}, u32[]{:S(2)}) async-start(s32[64,1,8]{2,1,0:T(1,128)} %copy.110), calls=%async_computation | async-start | bytes 65536 | tf_op jit(solution)/shard_map/all_to_all | solution.py:150
  229.3 67.9 %all-to-all-start.3 = ((bf16[64,8,2560]{2,1,0:T(8,128)(2,1)}), bf16[64,8,2560]{2,1,0:T(8,128)(2,1)S(1)}, u32[]{:S(2)}, u32[]{:S(2)}) async-start(bf16[64,8,2560]{2,1,0:T(8,128)(2,1)} %get-tuple-element.128), calls=%async_computation.3 | async-start | bytes 5242880 | tf_op jit(solution)/shard_map/all_to_all | solution.py:148
  306.4 5.7 %copy-start = (bf16[512,2560]{1,0:T(8,128)(2,1)S(1)}, bf16[512,2560]{1,0:T(8,128)(2,1)}, u32[]{:S(2)}) copy-start(bf16[512,2560]{1,0:T(8,128)(2,1)} %gather_fusion.1) | copy-start | bytes 7864324
  320.1 2.6 copy-start.1
  338.3 94.2 %all-to-all-start.4 = ((bf16[64,8,2560]{2,1,0:T(8,128)(2,1)}), bf16[64,8,2560]{2,1,0:T(8,128)(2,1)S(1)}, u32[]{:S(2)}, u32[]{:S(2)}) async-start(bf16[64,8,2560]{2,1,0:T(8,128)(2,1)} %bitcast_select_fusion), calls=%async_computation.4 | async-start | bytes 5242880 | tf_op jit(solution)/shard_map/all_to_all | solution.py:177
  347.8 9.1 %copy-start.2 = (bf16[128,2560]{1,0:T(8,128)(2,1)S(1)}, bf16[128,2560]{1,0:T(8,128)(2,1)}, u32[]{:S(2)}) copy-start(bf16[128,2560]{1,0:T(8,128)(2,1)} %get-tuple-element.138) | copy-start | bytes 1966084
  347.8 71.6 %collective-permute-start = (bf16[2,128,2560]{2,1,0:T(8,128)(2,1)}, bf16[2,128,2560]{2,1,0:T(8,128)(2,1)}, u32[]{:S(2)}, u32[]{:S(2)}) collective-permute-start(bf16[2,128,2560]{2,1,0:T(8,128)(2,1)} %pad_maximum_fusion), channel_id=1, source_target_pairs={{0,1},{1,2},{2,3},{3,4},{4,5},{5,6},{6,7},{7,8},{8,9},{9,10},{10,1... | collective-permute-start | bytes 3932168 | tf_op jit(solution)/shard_map/ppermute | solution.py:16
  428.1 1.1 copy-start.4
  428.1 1.3 copy-start.5
  440.1 29.0 %collective-permute-start.1 = (bf16[128,5120]{1,0:T(8,128)(2,1)S(1)}, bf16[128,5120]{1,0:T(8,128)(2,1)S(1)}, u32[]{:S(2)}, u32[]{:S(2)}) collective-permute-start(bf16[128,5120]{1,0:T(8,128)(2,1)S(1)} %pad_maximum_fusion.1), channel_id=1, source_target_pairs={{192,0},{0,64},{64,128},{128,192},{193,1},{1,65},{65,129},{129,193... | collective-permute-start | bytes 3932168 | tf_op jit(solution)/shard_map/ppermute | solution.py:35
where the time goes:
time: 480 us; the launch traced here: 471 us
  blocking collectives  183 us (38%)
  waiting for transfers between devices  126 us (26%)
  local copies, waits for them, and re-layouts  103 us (21%)
  starting transfers between devices  25.5 us (5%)
  other arithmetic  19.1 us (4%)
  matrix products  11.6 us (2%)
    all_to_all x1, blocking collectives, on_device(): lax.all_to_all(send_value, 'tok', split_axis=0, concat_axis=0, tiled=True)  71.9 us
    all_to_all x1, blocking collectives, on_device(): lax.all_to_all(send_query, 'tok', split_axis=0, concat_axis=0, tiled=True)  68.4 us
    ppermute x1, waiting for transfers between devices, passed_along(): return lax.ppermute(value, axis, pairs)  61.2 us
    all_gather x1, blocking collectives, prefix(): everything = lax.all_gather(value, axis)  42.3 us
    all_to_all x1, waiting for transfers between devices, on_device(): lax.all_to_all(send_key, 'tok', split_axis=0, concat_axis=0, tiled=True)  37.8 us
    ppermute x1, waiting for transfers between devices, shifted(): return lax.ppermute(block, axis, route)  27.4 us
    gather x3, local copies, waits for them, and re-layouts, arrange(): received.reshape(slot_total, half_width)[safe_slot]  20 us
    reshape x3, local copies, waits for them, and re-layouts, arrange(): received.reshape(slot_total, half_width)[safe_slot]  14.5 us
  transfers between devices with their start and end apart: 5, of which 3 were waited for; matrix products, arithmetic and copies ran while one was open for 14% of the time, Pallas kernels for 0%

commit v1 on v0

v1 whole, which is shorter than its diff:
```python
import functools
import math

import jax
import jax.numpy as jnp
from jax import lax
from jax.experimental import pallas as pl
from jax.experimental.pallas import tpu as pltpu
from jax.sharding import PartitionSpec as P

HD = 128
TOK = 128
HEADS = 20
HALF = HEADS * HD
PEERS = 64
CLUSTERS = 64
MOST = 8
SLOTS = PEERS * MOST
BLOCK = 256
LOW = -1e30
SCALE = math.log2(math.e) / math.sqrt(HD)
MESH = pl.DeviceIdType.MESH
BF16 = jnp.bfloat16
F32 = jnp.float32


def owner_of(head):
    pair = head // 5
    within = head % 5
    z = pair * 2 + within // 3
    y = head % 4
    return (y * 8 + z) * 2


def iota(shape, dim):
    return lax.broadcasted_iota(jnp.int32, shape, dim)


def dot(a, b, dims=((1,), (0,))):
    return lax.dot_general(a, b, (dims, ((), ())), preferred_element_type=F32)


def one_hot(hit):
    return jnp.where(hit, 1.0, 0.0).astype(BF16)


def layer_kernel(
    query, key, value, ids, out,
    meta, slots, qkbuf, vbuf, qe, ke, ve, bias0, bias1, split,
    lq, lk, lv, tails, lout,
    meta_send, meta_recv, bulk_send, qk_recv, v_recv, tail_send, tail_recv,
    load_sem, lout_send, back_send, out_recv, ready,
):
    s = lax.axis_index("section")
    t = lax.axis_index("tok")
    y, z, core = t // 16, (t // 2) % 8, t % 2
    first = (z // 2) * 5 + (z % 2) * 3
    offset = (y - first + 64) % 4
    head = first + offset
    is_owner = jnp.logical_and(offset < 3 - z % 2, core == 0)
    next_t, prev_t = (t + 1) % PEERS, (t + PEERS - 1) % PEERS
    next_s, prev_s = (s + 1) % 4, (s + 3) % 4

    barrier = pltpu.get_barrier_semaphore()

    @pl.when(is_owner)
    def _():
        @pl.loop(1, PEERS)
        def _(j):
            pl.semaphore_signal(
                barrier, inc=1, device_id=(s, (t + j) % PEERS), device_id_type=MESH
            )

    for peer in ((s, prev_t), (prev_s, t), (next_s, t)):
        pl.semaphore_signal(barrier, inc=1, device_id=peer, device_id_type=MESH)

    slots[...] = jnp.zeros_like(slots)
    col0, col1 = ids[:, 0:1], ids[:, 1:2]
    rows_at, cols_at = iota((TOK, TOK), 0), iota((TOK, TOK), 1)
    eye = rows_at == cols_at
    earlier = rows_at < cols_at
    for j, col in enumerate((col0, col1)):
        row = jnp.sum(jnp.where(eye, col, 0), axis=0, keepdims=True)
        same = jnp.logical_and(earlier, jnp.logical_or(col0 == row, col1 == row))
        rank = jnp.sum(jnp.where(same, 1, 0), axis=0, keepdims=True)
        slots[j : j + 1, :] = row * MOST + rank
    named = jnp.logical_or(col0 == cols_at, col1 == cols_at)
    slots[2:3, :] = jnp.sum(jnp.where(named, 1, 0), axis=0, keepdims=True)

    loads = [
        pltpu.make_async_copy(src.at[:, pl.ds(0, HALF)], dst, load_sem.at[a])
        for a, (src, dst) in enumerate(((query, lq), (key, lk), (value, lv)))
    ]
    for load in loads:
        load.start()

    pl.semaphore_wait(barrier, jnp.where(is_owner, HEADS - 1, HEADS) + 3)

    def spread(source, target, send, recv):
        @pl.loop(0, HEADS)
        def _(i):
            h = (i + first + core * 10) % HEADS
            owner = owner_of(h)

            @pl.when(owner != t)
            def _():
                pltpu.make_async_remote_copy(
                    src_ref=source(h), dst_ref=target, send_sem=send, recv_sem=recv,
                    device_id=(s, owner), device_id_type=MESH,
                ).start()

            @pl.when(owner == t)
            def _():
                pltpu.make_async_copy(source(h), target, recv).start()

    def head_block(array):
        return lambda h: array.at[:, pl.ds(pl.multiple_of(HALF + h * HD, HD), HD)]

    spread(lambda h: slots, meta.at[t], meta_send, meta_recv)
    tail_copies = [
        pltpu.make_async_remote_copy(
            src_ref=src.at[:, pl.ds(0, HALF)], dst_ref=tails.at[a],
            send_sem=tail_send.at[a], recv_sem=tail_recv.at[a],
            device_id=(s, next_t), device_id_type=MESH,
        )
        for a, src in enumerate((key, value))
    ]
    for copy in tail_copies:
        copy.start()
    spread(head_block(query), qkbuf.at[t, :, pl.ds(0, HD)], bulk_send.at[0], qk_recv)
    spread(head_block(key), qkbuf.at[t, :, pl.ds(HD, HD)], bulk_send.at[1], qk_recv)
    spread(head_block(value), vbuf.at[t], bulk_send.at[2], v_recv)

    @pl.when(is_owner)
    def _():
        pltpu.make_async_copy(meta, meta, meta_recv).wait()
        counts = meta[:, 2, :].astype(F32).astype(BF16)
        dev = iota((PEERS, SLOTS), 0)
        of_dev = iota((PEERS, SLOTS), 1) // MOST
        count = dot(counts, one_hot(dev == of_dev), ((0,), (0,)))
        before = dot(counts, one_hot(dev < of_dev), ((0,), (0,)))
        place = (iota((TOK, SLOTS), 1) % MOST).astype(F32)
        filled = place < count
        second = before + jnp.minimum(place, count) >= BLOCK
        bias0[...] = jnp.where(filled, 0.0, LOW)
        bias1[...] = jnp.where(jnp.logical_and(filled, second), 0.0, LOW)
        start = jnp.sum(jnp.where(second, 0.0, 1.0), axis=1, keepdims=True)
        split[...] = jnp.broadcast_to(start, (TOK, TOK))

    for load in loads:
        load.wait()
    for copy in tail_copies:
        copy.wait()

    @pl.loop(0, HEADS)
    def _(h):
        at = pl.ds(pl.multiple_of(h * HD, HD), HD)
        q_h = lq[:, at]
        before = dot(q_h, tails[0, :, at], ((1,), (1,))) * SCALE
        own = dot(q_h, lk[:, at], ((1,), (1,))) * SCALE
        reach = jnp.where(t == 0, TOK, 0)
        before = jnp.where(cols_at > rows_at + reach, before, LOW)
        own = jnp.where(cols_at <= rows_at, own, LOW)
        top = jnp.maximum(
            jnp.max(before, axis=1, keepdims=True), jnp.max(own, axis=1, keepdims=True)
        )
        before, own = jnp.exp2(before - top), jnp.exp2(own - top)
        total = jnp.sum(before + own, axis=1, keepdims=True)
        mixed = dot(before.astype(BF16), tails[1, :, at]) + dot(own.astype(BF16), lv[:, at])
        lout[:, at] = (mixed / total).astype(BF16)

    local_copy = pltpu.make_async_remote_copy(
        src_ref=lout, dst_ref=out.at[:, pl.ds(0, HALF)], send_sem=lout_send, recv_sem=out_recv,
        device_id=(next_s, t), device_id_type=MESH,
    )
    local_copy.start()

    @pl.when(is_owner)
    def _():
        slot_at = iota((SLOTS, TOK), 0)

        def members(d):
            return one_hot(
                jnp.logical_or(slot_at == meta[d, 0:1, :], slot_at == meta[d, 1:2, :])
            )

        def paired(a, b):
            width = a.shape[1]
            return jnp.concatenate(
                [a.reshape(CLUSTERS, MOST, width), b.reshape(CLUSTERS, MOST, width)], axis=1
            ).astype(BF16)

        pltpu.make_async_copy(qkbuf, qkbuf, qk_recv).wait()
        pl.semaphore_signal(ready, inc=1, device_id=(prev_s, t), device_id_type=MESH)

        @pl.loop(0, PEERS // 2)
        def _(i):
            at = pl.ds(pl.multiple_of(i * 2 * MOST, 2 * MOST), 2 * MOST)
            both = paired(dot(members(2 * i), qkbuf[2 * i]), dot(members(2 * i + 1), qkbuf[2 * i + 1]))
            qe[:, at, :] = both[:, :, :HD]
            ke[:, at, :] = both[:, :, HD:]

        pltpu.make_async_copy(vbuf, vbuf, v_recv).wait()

        @pl.loop(0, PEERS // 2)
        def _(i):
            at = pl.ds(pl.multiple_of(i * 2 * MOST, 2 * MOST), 2 * MOST)
            ve[:, at, :] = paired(dot(members(2 * i), vbuf[2 * i]), dot(members(2 * i + 1), vbuf[2 * i + 1]))

        pl.semaphore_wait(ready, 1)
        wide_at = iota((TOK, 2 * SLOTS), 1)
        for part in range(SLOTS // TOK):
            reach = (part + 1) * TOK

            @pl.loop(0, CLUSTERS)
            def _(c):
                q_c = qe[c, part * TOK : reach, :]
                scores = dot(q_c, ke[c, 0:reach, :], ((1,), (1,))) * SCALE
                row0, row1 = bias0[pl.ds(c, 1), :], bias1[pl.ds(c, 1), :]
                later = rows_at.astype(F32) + part * TOK >= split[pl.ds(c, 1), :]
                tiles = []
                for j in range(part + 1):
                    cut = slice(j * TOK, (j + 1) * TOK)
                    if part < BLOCK // TOK:
                        tile = scores[:, cut] + row0[:, cut]
                    else:
                        tile = scores[:, cut] + jnp.where(later, row1[:, cut], row0[:, cut])
                    if j == part:
                        tile = jnp.where(cols_at <= rows_at, tile, LOW)
                    tiles.append(tile)
                top = jnp.max(functools.reduce(jnp.maximum, tiles), axis=1, keepdims=True)
                tiles = [jnp.exp2(tile - top) for tile in tiles]
                total = jnp.sum(functools.reduce(jnp.add, tiles), axis=1, keepdims=True)
                weights = jnp.concatenate([tile.astype(BF16) for tile in tiles], axis=1)
                mixed = dot(weights, ve[c, 0:reach, :])
                qe[c, part * TOK : reach, :] = (mixed / total).astype(BF16)

            @pl.loop(part * 8, part * 8 + 8)
            def _(i):
                at = pl.ds(pl.multiple_of(i * 2 * MOST, 2 * MOST), 2 * MOST)
                rows = qe[:, at, :].reshape(2 * SLOTS, HD)
                for side in range(2):
                    d = 2 * i + side
                    hits = []
                    for j in range(2):
                        slot = meta[d, j : j + 1, :]
                        wide = (slot // MOST) * (2 * MOST) + slot % MOST + side * MOST
                        col = jnp.sum(jnp.where(eye, wide, 0), axis=1, keepdims=True)
                        hits.append(wide_at == col)
                    vbuf[d] = dot(one_hot(jnp.logical_or(*hits)), rows).astype(BF16)
                    pltpu.make_async_remote_copy(
                        src_ref=vbuf.at[d],
                        dst_ref=out.at[:, pl.ds(pl.multiple_of(HALF + head * HD, HD), HD)],
                        send_sem=back_send, recv_sem=out_recv,
                        device_id=(next_s, d), device_id_type=MESH,
                    ).start()

        pltpu.make_async_copy(vbuf, vbuf, back_send).wait()

    local_copy.wait_send()
    for sem, one in ((meta_send, None), (bulk_send.at[0], 0), (bulk_send.at[1], 0), (bulk_send.at[2], 0)):
        for many, mine in ((HEADS - 1, True), (HEADS, False)):
            @pl.when(is_owner if mine else jnp.logical_not(is_owner))
            def _():
                ref = meta.at[pl.ds(0, many)] if one is None else vbuf.at[pl.ds(0, many)]
                pltpu.make_async_copy(ref, ref, sem).wait()
    pltpu.make_async_copy(out, out, out_recv).wait()


def on_device(queries, keys, values, cluster_ids):
    any_space = pl.BlockSpec(memory_space=pl.ANY)
    vmem = pltpu.VMEM
    expanded = vmem((CLUSTERS, SLOTS, HD), BF16)
    wide = vmem((TOK, HALF), BF16)
    dma = pltpu.SemaphoreType.DMA
    layer = pl.pallas_call(
        layer_kernel,
        out_shape=jax.ShapeDtypeStruct((TOK, 2 * HALF), BF16),
        in_specs=[any_space] * 3 + [pl.BlockSpec(memory_space=vmem)],
        out_specs=any_space,
        scratch_shapes=[
            vmem((PEERS, 8, TOK), jnp.int32),
            vmem((8, TOK), jnp.int32),
            vmem((PEERS, TOK, 2 * HD), BF16),
            vmem((PEERS, TOK, HD), BF16),
            expanded, expanded, expanded,
            vmem((TOK, SLOTS), F32),
            vmem((TOK, SLOTS), F32),
            vmem((TOK, TOK), F32),
            wide, wide, wide,
            vmem((2, TOK, HALF), BF16),
            wide,
            dma, dma, dma((3,)), dma, dma, dma((2,)), dma((2,)),
            dma((3,)), dma, dma, dma, pltpu.SemaphoreType.REGULAR,
        ],
        compiler_params=pltpu.CompilerParams(
            collective_id=0, has_side_effects=True, vmem_limit_bytes=60 << 20
        ),
    )(queries[0], keys[0], values[0], cluster_ids[0])
    return layer[None]


def solution(mesh):
    spec = P("section", "tok", None)
    return jax.shard_map(
        on_device, mesh=mesh, in_specs=(spec,) * 4, out_specs=spec, check_vma=False
    )
```

time: 480 us -> 222 us (0.46)
  the two profiles are of different devices: /device:TPU:8 before, /device:TPU:25 now
where the time goes in v1:
time: 222 us; the launch traced here: 220 us
  Pallas kernels  216 us (97%)
  local copies, waits for them, and re-layouts  3.87 us (2%)
    pallas_call x1, Pallas kernels, on_device(): pl.pallas_call(layer_kernel, out_shape=jax.ShapeDtypeStruct((TOK, 2 * HAL...  216 us

profile of v1, /device:TPU:25, one launch (start us, length us, event | category | flops | bytes accessed | tf_op | source)
XLA Modules:
  0.0 220.2 jit_solution(18093438922861809657)
XLA Ops:
  0.0 1.4 copy.5
  1.4 216.3 %shard_map.46 = bf16[128,5120]{1,0:T(8,128)(2,1)} custom-call(bf16[128,5120]{1,0:T(8,128)(2,1)} %bitcast.6, bf16[128,5120]{1,0:T(8,128)(2,1)} %bitcast.7, bf16[128,5120]{1,0:T(8,128)(2,1)} %bitcast.8, s32[128,2]{1,0:T(8,128)} %bitcast.9), custom_call_target="tpu_custom_call" | custom-call | tf_op jit(solution)/shard_map/pallas_call | solution.py:276
  217.7 2.5 %copy.7 = bf16[1,128,5120]{2,1,0:T(8,128)(2,1)} copy(bf16[1,128,5120]{2,1,0:T(8,128)(2,1)} %bitcast.5) | data formatting | bytes 2621440

commit v2 on v1

--- a/solution.py
+++ b/solution.py
@@ -15,6 +15,8 @@
 PEERS = 64
 CLUSTERS = 64
 MOST = 8
+GROUP = 8
+LOCAL_GROUP = 5
 SLOTS = PEERS * MOST
 BLOCK = 256
 LOW = -1e30
@@ -46,7 +48,7 @@
 
 def layer_kernel(
     query, key, value, ids, out,
-    meta, slots, qkbuf, vbuf, qe, ke, ve, bias0, bias1, split,
+    meta, slots, qkbuf, vbuf, hot, qe, ke, ve, bias0, bias1, split,
     lq, lk, lv, tails, lout,
     meta_send, meta_recv, bulk_send, qk_recv, v_recv, tail_send, tail_recv,
     load_sem, lout_send, back_send, out_recv, ready,
@@ -142,32 +144,46 @@
         place = (iota((TOK, SLOTS), 1) % MOST).astype(F32)
         filled = place < count
         second = before + jnp.minimum(place, count) >= BLOCK
-        bias0[...] = jnp.where(filled, 0.0, LOW)
-        bias1[...] = jnp.where(jnp.logical_and(filled, second), 0.0, LOW)
+        def by_cluster(array):
+            return array[:CLUSTERS].reshape(CLUSTERS, 1, array.shape[1])
+
+        bias0[...] = by_cluster(jnp.where(filled, 0.0, LOW))
+        bias1[...] = by_cluster(jnp.where(jnp.logical_and(filled, second), 0.0, LOW))
         start = jnp.sum(jnp.where(second, 0.0, 1.0), axis=1, keepdims=True)
-        split[...] = jnp.broadcast_to(start, (TOK, TOK))
+        split[...] = by_cluster(jnp.broadcast_to(start, (TOK, TOK)))
 
     for load in loads:
         load.wait()
     for copy in tail_copies:
         copy.wait()
 
-    @pl.loop(0, HEADS)
-    def _(h):
-        at = pl.ds(pl.multiple_of(h * HD, HD), HD)
-        q_h = lq[:, at]
-        before = dot(q_h, tails[0, :, at], ((1,), (1,))) * SCALE
-        own = dot(q_h, lk[:, at], ((1,), (1,))) * SCALE
-        reach = jnp.where(t == 0, TOK, 0)
-        before = jnp.where(cols_at > rows_at + reach, before, LOW)
-        own = jnp.where(cols_at <= rows_at, own, LOW)
-        top = jnp.maximum(
-            jnp.max(before, axis=1, keepdims=True), jnp.max(own, axis=1, keepdims=True)
-        )
-        before, own = jnp.exp2(before - top), jnp.exp2(own - top)
-        total = jnp.sum(before + own, axis=1, keepdims=True)
-        mixed = dot(before.astype(BF16), tails[1, :, at]) + dot(own.astype(BF16), lv[:, at])
-        lout[:, at] = (mixed / total).astype(BF16)
+    reach = jnp.where(t == 0, TOK, 0)
+    window = cols_at > rows_at + reach
+    causal = cols_at <= rows_at
+
+    @pl.loop(0, HEADS // LOCAL_GROUP)
+    def _(g):
+        ats = [
+            pl.ds(pl.multiple_of((g * LOCAL_GROUP + i) * HD, HD), HD) for i in range(LOCAL_GROUP)
+        ]
+        scores = [
+            (dot(lq[:, at], tails[0, :, at], ((1,), (1,))), dot(lq[:, at], lk[:, at], ((1,), (1,))))
+            for at in ats
+        ]
+        parts = []
+        for before, own in scores:
+            before = jnp.where(window, before * SCALE, LOW)
+            own = jnp.where(causal, own * SCALE, LOW)
+            top = jnp.max(jnp.maximum(before, own), axis=1, keepdims=True)
+            before, own = jnp.exp2(before - top), jnp.exp2(own - top)
+            total = jnp.sum(before + own, axis=1, keepdims=True)
+            parts.append((before.astype(BF16), own.astype(BF16), total))
+        mixed = [
+            (dot(before, tails[1, :, at]) + dot(own, lv[:, at])) / total
+            for at, (before, own, total) in zip(ats, parts)
+        ]
+        for at, mix in zip(ats, mixed):
+            lout[:, at] = mix.astype(BF16)
 
     local_copy = pltpu.make_async_remote_copy(
         src_ref=lout, dst_ref=out.at[:, pl.ds(0, HALF)], send_sem=lout_send, recv_sem=out_recv,
@@ -193,66 +209,80 @@
         pltpu.make_async_copy(qkbuf, qkbuf, qk_recv).wait()
         pl.semaphore_signal(ready, inc=1, device_id=(prev_s, t), device_id_type=MESH)
 
-        @pl.loop(0, PEERS // 2)
-        def _(i):
-            at = pl.ds(pl.multiple_of(i * 2 * MOST, 2 * MOST), 2 * MOST)
-            both = paired(dot(members(2 * i), qkbuf[2 * i]), dot(members(2 * i + 1), qkbuf[2 * i + 1]))
-            qe[:, at, :] = both[:, :, :HD]
-            ke[:, at, :] = both[:, :, HD:]
+        def pair_at(i):
+            return pl.ds(pl.multiple_of(i * 2 * MOST, 2 * MOST), 2 * MOST)
+
+        @pl.loop(0, PEERS // 4)
+        def _(g):
+            products = []
+            for i in range(4):
+                hits = members(g * 4 + i)
+                hot[g * 4 + i] = hits
+                products.append(dot(hits, qkbuf[g * 4 + i]))
+            for i in range(2):
+                both = paired(products[2 * i], products[2 * i + 1])
+                qe[:, pair_at(g * 2 + i), :] = both[:, :, :HD]
+                ke[:, pair_at(g * 2 + i), :] = both[:, :, HD:]
 
         pltpu.make_async_copy(vbuf, vbuf, v_recv).wait()
 
-        @pl.loop(0, PEERS // 2)
-        def _(i):
-            at = pl.ds(pl.multiple_of(i * 2 * MOST, 2 * MOST), 2 * MOST)
-            ve[:, at, :] = paired(dot(members(2 * i), vbuf[2 * i]), dot(members(2 * i + 1), vbuf[2 * i + 1]))
+        @pl.loop(0, PEERS // 8)
+        def _(g):
+            products = [dot(hot[g * 8 + i], vbuf[g * 8 + i]) for i in range(8)]
+            for i in range(4):
+                ve[:, pair_at(g * 4 + i), :] = paired(products[2 * i], products[2 * i + 1])
 
         pl.semaphore_wait(ready, 1)
-        wide_at = iota((TOK, 2 * SLOTS), 1)
         for part in range(SLOTS // TOK):
-            reach = (part + 1) * TOK
-
-            @pl.loop(0, CLUSTERS)
-            def _(c):
-                q_c = qe[c, part * TOK : reach, :]
-                scores = dot(q_c, ke[c, 0:reach, :], ((1,), (1,))) * SCALE
-                row0, row1 = bias0[pl.ds(c, 1), :], bias1[pl.ds(c, 1), :]
-                later = rows_at.astype(F32) + part * TOK >= split[pl.ds(c, 1), :]
+            lo, hi = part * TOK, (part + 1) * TOK
+
+            def soften(scores, c):
+                row0, row1 = bias0[c, :, :hi], bias1[c, :, :hi]
+                later = rows_at.astype(F32) + lo >= split[c]
                 tiles = []
                 for j in range(part + 1):
                     cut = slice(j * TOK, (j + 1) * TOK)
-                    if part < BLOCK // TOK:
-                        tile = scores[:, cut] + row0[:, cut]
-                    else:
-                        tile = scores[:, cut] + jnp.where(later, row1[:, cut], row0[:, cut])
+                    bias = row0[:, cut]
+                    if part >= BLOCK // TOK:
+                        bias = jnp.where(later, row1[:, cut], bias)
+                    tile = scores[:, cut] * SCALE + bias
                     if j == part:
-                        tile = jnp.where(cols_at <= rows_at, tile, LOW)
+                        tile = jnp.where(causal, tile, LOW)
                     tiles.append(tile)
                 top = jnp.max(functools.reduce(jnp.maximum, tiles), axis=1, keepdims=True)
                 tiles = [jnp.exp2(tile - top) for tile in tiles]
                 total = jnp.sum(functools.reduce(jnp.add, tiles), axis=1, keepdims=True)
-                weights = jnp.concatenate([tile.astype(BF16) for tile in tiles], axis=1)
-                mixed = dot(weights, ve[c, 0:reach, :])
-                qe[c, part * TOK : reach, :] = (mixed / total).astype(BF16)
-
-            @pl.loop(part * 8, part * 8 + 8)
-            def _(i):
-                at = pl.ds(pl.multiple_of(i * 2 * MOST, 2 * MOST), 2 * MOST)
-                rows = qe[:, at, :].reshape(2 * SLOTS, HD)
-                for side in range(2):
-                    d = 2 * i + side
-                    hits = []
-                    for j in range(2):
-                        slot = meta[d, j : j + 1, :]
-                        wide = (slot // MOST) * (2 * MOST) + slot % MOST + side * MOST
-                        col = jnp.sum(jnp.where(eye, wide, 0), axis=1, keepdims=True)
-                        hits.append(wide_at == col)
-                    vbuf[d] = dot(one_hot(jnp.logical_or(*hits)), rows).astype(BF16)
+                return jnp.concatenate([tile.astype(BF16) for tile in tiles], axis=1), total
+
+            @pl.loop(0, CLUSTERS // GROUP)
+            def _(g):
+                clusters = [g * GROUP + i for i in range(GROUP)]
+                scores = [dot(qe[c, lo:hi, :], ke[c, 0:hi, :], ((1,), (1,))) for c in clusters]
+                weights = [soften(score, c) for score, c in zip(scores, clusters)]
+                mixed = [
+                    (dot(weight, ve[c, 0:hi, :]) / total).astype(BF16)
+                    for (weight, total), c in zip(weights, clusters)
+                ]
+                for c, mix in zip(clusters, mixed):
+                    qe[c, lo:hi, :] = mix
+
+            @pl.loop(part * 2, part * 2 + 2)
+            def _(g):
+                sums = []
+                for i in range(4):
+                    rows = qe[:, pair_at(g * 4 + i), :].astype(F32)
+                    for side in range(2):
+                        slot_rows = rows[:, side * MOST : (side + 1) * MOST, :]
+                        slot_rows = slot_rows.reshape(SLOTS, HD).astype(BF16)
+                        sums.append(dot(hot[g * 8 + 2 * i + side], slot_rows, ((0,), (0,))).astype(BF16))
+                for i in range(8):
+                    vbuf[g * 8 + i] = sums[i]
+                for i in range(8):
                     pltpu.make_async_remote_copy(
-                        src_ref=vbuf.at[d],
+                        src_ref=vbuf.at[g * 8 + i],
                         dst_ref=out.at[:, pl.ds(pl.multiple_of(HALF + head * HD, HD), HD)],
                         send_sem=back_send, recv_sem=out_recv,
-                        device_id=(next_s, d), device_id_type=MESH,
+                        device_id=(next_s, g * 8 + i), device_id_type=MESH,
                     ).start()
 
         pltpu.make_async_copy(vbuf, vbuf, back_send).wait()
@@ -283,10 +313,11 @@
             vmem((8, TOK), jnp.int32),
             vmem((PEERS, TOK, 2 * HD), BF16),
             vmem((PEERS, TOK, HD), BF16),
+            vmem((PEERS, SLOTS, TOK), BF16),
             expanded, expanded, expanded,
-            vmem((TOK, SLOTS), F32),
-            vmem((TOK, SLOTS), F32),
-            vmem((TOK, TOK), F32),
+            vmem((CLUSTERS, 1, SLOTS), F32),
+            vmem((CLUSTERS, 1, SLOTS), F32),
+            vmem((CLUSTERS, 1, TOK), F32),
             wide, wide, wide,
             vmem((2, TOK, HALF), BF16),
             wide,

time: 222 us -> 126 us (0.57)
  Pallas kernels: 216 us -> 122 us
    pallas_call x1, Pallas kernels: 216 us -> 122 us  [on_device(): pl.pallas_call(layer_kernel, out_shape=jax.ShapeDtypeStruct((TOK, 2 * HAL...]
where the time goes in v2:
time: 126 us; the launch traced here: 125 us
  Pallas kernels  122 us (97%)
  local copies, waits for them, and re-layouts  3.87 us (3%)
    pallas_call x1, Pallas kernels, on_device(): pl.pallas_call(layer_kernel, out_shape=jax.ShapeDtypeStruct((TOK, 2 * HAL...  122 us
    unnamed x2, local copies, waits for them, and re-layouts  3.87 us

profile of v2, /device:TPU:25, one launch (start us, length us, event | category | flops | bytes accessed | tf_op | source)
XLA Modules:
  0.0 125.5 jit_solution(9850615084023505219)
XLA Ops:
  0.0 1.4 %copy.5 = s32[1,128,2]{2,1,0:T(8,128)} copy(s32[1,128,2]{1,2,0:T(2,128)} %param.7) | data formatting | bytes 2048 | tf_op args[3]
  1.4 121.6 %shard_map.46 = bf16[128,5120]{1,0:T(8,128)(2,1)} custom-call(bf16[128,5120]{1,0:T(8,128)(2,1)} %bitcast.6, bf16[128,5120]{1,0:T(8,128)(2,1)} %bitcast.7, bf16[128,5120]{1,0:T(8,128)(2,1)} %bitcast.8, s32[128,2]{1,0:T(8,128)} %bitcast.9), custom_call_target="tpu_custom_call" | custom-call | tf_op jit(solution)/shard_map/pallas_call | solution.py:306
  123.0 2.5 %copy.7 = bf16[1,128,5120]{2,1,0:T(8,128)(2,1)} copy(bf16[1,128,5120]{2,1,0:T(8,128)(2,1)} %bitcast.5) | data formatting | bytes 2621440

commit v3 on v2

v3 whole, which is shorter than its diff:
```python
import functools
import math

import jax
import jax.numpy as jnp
from jax import lax
from jax.experimental import pallas as pl
from jax.experimental.pallas import tpu as pltpu
from jax.sharding import PartitionSpec as P

HD = 128
TOK = 128
HEADS = 20
HALF = HEADS * HD
PEERS = 64
CLUSTERS = 64
MOST = 8
LOCAL_GROUP = 5
EARLY = 10
SLOTS = PEERS * MOST
PARTS = SLOTS // TOK
GROUPS = (16, 16, 8, 8)
BLOCK = 256
LOW = -1e30
SCALE = math.log2(math.e) / math.sqrt(HD)
MESH = pl.DeviceIdType.MESH
BF16 = jnp.bfloat16
F32 = jnp.float32


def owner_of(head):
    pair = head // 5
    within = head % 5
    z = pair * 2 + within // 3
    y = head % 4
    return (y * 8 + z) * 2 + 1


def iota(shape, dim):
    return lax.broadcasted_iota(jnp.int32, shape, dim)


def dot(a, b, dims=((1,), (0,))):
    return lax.dot_general(a, b, (dims, ((), ())), preferred_element_type=F32)


def one_hot(hit):
    return jnp.where(hit, 1.0, 0.0).astype(BF16)


def layer_kernel(
    query, key, value, ids, out,
    meta, slots, qbuf, kbuf, vbuf, hot, qe, ke, weights0, weights1, weights2, weights3,
    bias0, bias1, split, lq, lk, lv, tails, lout,
    meta_send, meta_recv, bulk_send, q_recv, k_recv, v_recv, tail_send, tail_recv,
    load_sem, lout_send, back_send, out_recv, ready,
):
    s = lax.axis_index("section")
    t = lax.axis_index("tok")
    y, z, core = t // 16, (t // 2) % 8, t % 2
    first = (z // 2) * 5 + (z % 2) * 3
    offset = (y - first + 64) % 4
    head = first + offset
    is_owner = jnp.logical_and(offset < 3 - z % 2, core == 1)
    next_t, prev_t = (t + 1) % PEERS, (t + PEERS - 1) % PEERS
    next_s, prev_s = (s + 1) % 4, (s + 3) % 4

    barrier = pltpu.get_barrier_semaphore()

    @pl.when(is_owner)
    def _():
        @pl.loop(1, PEERS)
        def _(j):
            pl.semaphore_signal(
                barrier, inc=1, device_id=(s, (t + j) % PEERS), device_id_type=MESH
            )

    for peer in ((s, prev_t), (prev_s, t), (next_s, t)):
        pl.semaphore_signal(barrier, inc=1, device_id=peer, device_id_type=MESH)

    slots[...] = jnp.zeros_like(slots)
    rows_at, cols_at = iota((TOK, TOK), 0), iota((TOK, TOK), 1)
    eye = rows_at == cols_at
    earlier = rows_at < cols_at
    picks = [ids[j : j + 1, :] for j in range(2)]
    col0, col1 = [jnp.sum(jnp.where(eye, row, 0), axis=1, keepdims=True) for row in picks]
    for j, row in enumerate(picks):
        same = jnp.logical_and(earlier, jnp.logical_or(col0 == row, col1 == row))
        rank = jnp.sum(jnp.where(same, 1, 0), axis=0, keepdims=True)
        slots[j : j + 1, :] = row * MOST + rank
    named = jnp.logical_or(col0 == cols_at, col1 == cols_at)
    slots[2:3, :] = jnp.sum(jnp.where(named, 1, 0), axis=0, keepdims=True)

    loads = [
        pltpu.make_async_copy(src.at[:, pl.ds(0, HALF)], dst, load_sem.at[a])
        for a, (src, dst) in enumerate(((query, lq), (key, lk), (value, lv)))
    ]
    for load in loads:
        load.start()

    pl.semaphore_wait(barrier, jnp.where(is_owner, HEADS - 1, HEADS) + 3)

    def spread(source, target, send, recv):
        @pl.loop(0, HEADS)
        def _(i):
            step = jnp.where(i % 2 == 0, i // 2, HEADS - 1 - i // 2)
            h = (first + step) % HEADS
            owner = owner_of(h)

            @pl.when(owner != t)
            def _():
                pltpu.make_async_remote_copy(
                    src_ref=source(h), dst_ref=target, send_sem=send, recv_sem=recv,
                    device_id=(s, owner), device_id_type=MESH,
                ).start()

            @pl.when(owner == t)
            def _():
                pltpu.make_async_copy(source(h), target, recv).start()

    def head_block(array):
        return lambda h: array.at[:, pl.ds(pl.multiple_of(HALF + h * HD, HD), HD)]

    def columns(half):
        return pl.ds(half * EARLY * HD, (EARLY if half == 0 else HEADS - EARLY) * HD)

    def tail_copies(half):
        return [
            pltpu.make_async_remote_copy(
                src_ref=src.at[:, columns(half)], dst_ref=tails.at[a, :, columns(half)],
                send_sem=tail_send.at[half, a], recv_sem=tail_recv.at[half, a],
                device_id=(s, next_t), device_id_type=MESH,
            )
            for a, src in enumerate((key, value))
        ]

    def start_tails(half):
        for copy in tail_copies(half):
            copy.start()

    spread(lambda h: slots, meta.at[t], meta_send, meta_recv)
    start_tails(0)

    @pl.when(core == 0)
    def _():
        start_tails(1)

    spread(head_block(query), qbuf.at[t], bulk_send.at[0], q_recv.at[z])
    spread(head_block(key), kbuf.at[t], bulk_send.at[1], k_recv.at[z])

    def await_sends(sem, buf):
        for many, mine in ((HEADS - 1, True), (HEADS, False)):

            @pl.when(is_owner if mine else jnp.logical_not(is_owner))
            def _():
                ref = buf.at[pl.ds(0, many)]
                pltpu.make_async_copy(ref, ref, sem).wait()

    @pl.when(is_owner)
    def _():
        pltpu.make_async_copy(meta, meta, meta_recv).wait()
        counts = meta[:, 2, :].astype(F32).astype(BF16)
        dev = iota((PEERS, SLOTS), 0)
        of_dev = iota((PEERS, SLOTS), 1) // MOST
        count = dot(counts, one_hot(dev == of_dev), ((0,), (0,)))
        before = dot(counts, one_hot(dev < of_dev), ((0,), (0,)))
        place = (iota((TOK, SLOTS), 1) % MOST).astype(F32)
        filled = place < count
        second = before + jnp.minimum(place, count) >= BLOCK
        def by_cluster(array):
            return array[:CLUSTERS].reshape(CLUSTERS, 1, array.shape[1])

        slot_at = iota((SLOTS, TOK), 0)

        @pl.loop(0, PEERS // 4)
        def _(g):
            for i in range(4):
                d = g * 4 + i
                hot[d] = one_hot(
                    jnp.logical_or(slot_at == meta[d, 0:1, :], slot_at == meta[d, 1:2, :])
                )

        bias0[...] = by_cluster(jnp.where(filled, 0.0, LOW))
        bias1[...] = by_cluster(jnp.where(jnp.logical_and(filled, second), 0.0, LOW))
        start = jnp.sum(jnp.where(second, 0.0, 1.0), axis=1, keepdims=True)
        split[...] = by_cluster(jnp.broadcast_to(start, (TOK, TOK)))

    reach = jnp.where(t == 0, TOK, 0)
    window = cols_at > rows_at + reach
    causal = cols_at <= rows_at

    def local_copy(half):
        return pltpu.make_async_remote_copy(
            src_ref=lout.at[:, columns(half)], dst_ref=out.at[:, columns(half)],
            send_sem=lout_send.at[half], recv_sem=out_recv,
            device_id=(next_s, t), device_id_type=MESH,
        )

    def local_heads(half):
        for copy in tail_copies(half):
            copy.wait_recv()
        lo, hi = (0, EARLY) if half == 0 else (EARLY, HEADS)

        @pl.loop(lo // LOCAL_GROUP, hi // LOCAL_GROUP)
        def _(g):
            ats = [
                pl.ds(pl.multiple_of((g * LOCAL_GROUP + i) * HD, HD), HD)
                for i in range(LOCAL_GROUP)
            ]
            scores = [
                (dot(lq[:, at], tails[0, :, at], ((1,), (1,))), dot(lq[:, at], lk[:, at], ((1,), (1,))))
                for at in ats
            ]
            parts = []
            for before, own in scores:
                before = jnp.where(window, before * SCALE, LOW)
                own = jnp.where(causal, own * SCALE, LOW)
                top = jnp.max(jnp.maximum(before, own), axis=1, keepdims=True)
                before, own = jnp.exp2(before - top), jnp.exp2(own - top)
                total = jnp.sum(before + own, axis=1, keepdims=True)
                parts.append((before.astype(BF16), own.astype(BF16), total))
            mixed = [
                (dot(before, tails[1, :, at]) + dot(own, lv[:, at])) / total
                for at, (before, own, total) in zip(ats, parts)
            ]
            for at, mix in zip(ats, mixed):
                lout[:, at] = mix.astype(BF16)

        local_copy(half).start()

    for load in loads:
        load.wait()
    local_heads(0)

    @pl.when(core == 1)
    def _():
        local_heads(1)

    await_sends(bulk_send.at[0], vbuf)
    @pl.when(core == 1)
    def _():
        start_tails(1)
    spread(head_block(value), vbuf.at[t], bulk_send.at[2], v_recv.at[z])


    @pl.when(is_owner)
    def _():
        def paired(a, b):
            width = a.shape[1]
            return jnp.concatenate(
                [a.reshape(CLUSTERS, MOST, width), b.reshape(CLUSTERS, MOST, width)], axis=1
            ).astype(BF16)

        def pair_at(i):
            return pl.ds(pl.multiple_of(i * 2 * MOST, 2 * MOST), 2 * MOST)

        def expand(buf, recv, target):
            @pl.loop(0, 8)
            def _(i):
                ahead = jnp.where(i % 2 == 1, (i + 1) // 2, 8 - i // 2)
                at_z = (z + ahead) % 8
                group = buf.at[pl.ds(0, 8)]
                pltpu.make_async_copy(group, group, recv.at[at_z]).wait()
                sources = [at_y * 16 + at_z * 2 + c for at_y in range(4) for c in range(2)]
                products = [dot(hot[d], buf[d]) for d in sources]
                for at_y in range(4):
                    target[:, pair_at(at_y * 8 + at_z), :] = paired(
                        products[2 * at_y], products[2 * at_y + 1]
                    )

        expand(qbuf, q_recv, qe)
        pl.semaphore_signal(ready, inc=1, device_id=(prev_s, t), device_id_type=MESH)
        expand(kbuf, k_recv, ke)

        stored = (weights0, weights1, weights2, weights3)
        for part in range(PARTS):
            lo, hi = part * TOK, (part + 1) * TOK

            def soften(scores, c):
                row0, row1 = bias0[c, :, :hi], bias1[c, :, :hi]
                later = rows_at.astype(F32) + lo >= split[c]
                tiles = []
                for j in range(part + 1):
                    cut = slice(j * TOK, (j + 1) * TOK)
                    bias = row0[:, cut]
                    if part >= BLOCK // TOK:
                        bias = jnp.where(later, row1[:, cut], bias)
                    tile = scores[:, cut] * SCALE + bias
                    if j == part:
                        tile = jnp.where(causal, tile, LOW)
                    tiles.append(tile)
                top = jnp.max(functools.reduce(jnp.maximum, tiles), axis=1, keepdims=True)
                return jnp.concatenate([jnp.exp2(tile - top).astype(BF16) for tile in tiles], axis=1)

            @pl.loop(0, CLUSTERS // GROUPS[part])
            def _(g):
                clusters = [g * GROUPS[part] + i for i in range(GROUPS[part])]
                scores = [dot(qe[c, lo:hi, :], ke[c, 0:hi, :], ((1,), (1,))) for c in clusters]
                weights = [soften(score, c) for score, c in zip(scores, clusters)]
                for c, weight in zip(clusters, weights):
                    stored[part][c] = weight

        expand(vbuf, v_recv, ke)
        pl.semaphore_wait(ready, 1)
        ones = jnp.ones((SLOTS, HD), BF16)
        for part in range(PARTS):
            lo, hi = part * TOK, (part + 1) * TOK

            @pl.loop(0, CLUSTERS // GROUPS[part])
            def _(g):
                clusters = [g * GROUPS[part] + i for i in range(GROUPS[part])]
                mixed = []
                for c in clusters:
                    operand = jnp.concatenate([ke[c, 0:hi, :], ones[:hi]], axis=1)
                    product = dot(stored[part][c], operand)
                    mixed.append((product[:, :HD] / product[:, HD:]).astype(BF16))
                for c, mix in zip(clusters, mixed):
                    qe[c, lo:hi, :] = mix

            @pl.loop(part * 2, part * 2 + 2)
            def _(g):
                sums = []
                for i in range(4):
                    rows = qe[:, pair_at(g * 4 + i), :].astype(F32)
                    for side in range(2):
                        slot_rows = rows[:, side * MOST : (side + 1) * MOST, :]
                        slot_rows = slot_rows.reshape(SLOTS, HD).astype(BF16)
                        sums.append(dot(hot[g * 8 + 2 * i + side], slot_rows, ((0,), (0,))).astype(BF16))
                for i in range(8):
                    vbuf[g * 8 + i] = sums[i]
                for i in range(8):
                    pltpu.make_async_remote_copy(
                        src_ref=vbuf.at[g * 8 + i],
                        dst_ref=out.at[:, pl.ds(pl.multiple_of(HALF + head * HD, HD), HD)],
                        send_sem=back_send, recv_sem=out_recv,
                        device_id=(next_s, g * 8 + i), device_id_type=MESH,
                    ).start()

        pltpu.make_async_copy(vbuf, vbuf, back_send).wait()

    @pl.when(core == 0)
    def _():
        local_heads(1)

    for half in range(2):
        local_copy(half).wait_send()
        for copy in tail_copies(half):
            copy.wait_send()
    await_sends(meta_send, meta)
    await_sends(bulk_send.at[1], vbuf)
    await_sends(bulk_send.at[2], vbuf)
    pltpu.make_async_copy(out, out, out_recv).wait()


def on_device(queries, keys, values, cluster_ids):
    any_space = pl.BlockSpec(memory_space=pl.ANY)
    vmem = pltpu.VMEM
    expanded = vmem((CLUSTERS, SLOTS, HD), BF16)
    wide = vmem((TOK, HALF), BF16)
    dma = pltpu.SemaphoreType.DMA
    layer = pl.pallas_call(
        layer_kernel,
        out_shape=jax.ShapeDtypeStruct((TOK, 2 * HALF), BF16),
        in_specs=[any_space] * 3 + [pl.BlockSpec(memory_space=vmem)],
        out_specs=any_space,
        scratch_shapes=[
            vmem((PEERS, 8, TOK), jnp.int32),
            vmem((8, TOK), jnp.int32),
            vmem((PEERS, TOK, HD), BF16),
            vmem((PEERS, TOK, HD), BF16),
            vmem((PEERS, TOK, HD), BF16),
            vmem((PEERS, SLOTS, TOK), BF16),
            expanded, expanded,
            *(vmem((CLUSTERS, TOK, (part + 1) * TOK), BF16) for part in range(PARTS)),
            vmem((CLUSTERS, 1, SLOTS), F32),
            vmem((CLUSTERS, 1, SLOTS), F32),
            vmem((CLUSTERS, 1, TOK), F32),
            wide, wide, wide,
            vmem((2, TOK, HALF), BF16),
            wide,
            dma, dma, dma((3,)), dma((8,)), dma((8,)), dma((8,)), dma((2, 2)), dma((2, 2)),
            dma((3,)), dma((2,)), dma, dma, pltpu.SemaphoreType.REGULAR,
        ],
        compiler_params=pltpu.CompilerParams(
            collective_id=0, has_side_effects=True, vmem_limit_bytes=60 << 20
        ),
    )(queries[0], keys[0], values[0], cluster_ids[0].T)
    return layer[None]


def solution(mesh):
    spec = P("section", "tok", None)
    return jax.shard_map(
        on_device, mesh=mesh, in_specs=(spec,) * 4, out_specs=spec, check_vma=False
    )
```

time: 126 us -> 109 us (0.87)
  Pallas kernels: 122 us -> 106 us
  local copies, waits for them, and re-layouts: 3.87 us -> 2.46 us
    pallas_call x1, Pallas kernels: 122 us -> 106 us  [on_device(): pl.pallas_call(layer_kernel, out_shape=jax.ShapeDtypeStruct((TOK, 2 * HAL...]
    unnamed x2 -> x1, local copies, waits for them, and re-layouts: 3.87 us -> 2.46 us
where the time goes in v3:
time: 109 us; the launch traced here: 108 us
  Pallas kernels  106 us (97%)
  local copies, waits for them, and re-layouts  2.46 us (2%)
    pallas_call x1, Pallas kernels, on_device(): pl.pallas_call(layer_kernel, out_shape=jax.ShapeDtypeStruct((TOK, 2 * HAL...  106 us
    unnamed x1, local copies, waits for them, and re-layouts  2.46 us

profile of v3, /device:TPU:25, one launch (start us, length us, event | category | flops | bytes accessed | tf_op | source)
XLA Modules:
  0.0 108.4 jit_solution(11890380928579654819)
XLA Ops:
  0.0 105.9 %shard_map.46 = bf16[128,5120]{1,0:T(8,128)(2,1)} custom-call(bf16[128,5120]{1,0:T(8,128)(2,1)} %bitcast.8, bf16[128,5120]{1,0:T(8,128)(2,1)} %bitcast.9, bf16[128,5120]{1,0:T(8,128)(2,1)} %bitcast.10, s32[2,128]{1,0:T(2,128)} %bitcast.11), custom_call_target="tpu_custom_call" | custom-call | tf_op jit(solution)/shard_map/pallas_call | solution.py:361
  105.9 2.5 %copy.6 = bf16[1,128,5120]{2,1,0:T(8,128)(2,1)} copy(bf16[1,128,5120]{2,1,0:T(8,128)(2,1)} %bitcast.7) | data formatting | bytes 2621440

commit v4 on v3

--- a/solution.py
+++ b/solution.py
@@ -16,7 +16,6 @@
 CLUSTERS = 64
 MOST = 8
 LOCAL_GROUP = 5
-EARLY = 10
 SLOTS = PEERS * MOST
 PARTS = SLOTS // TOK
 GROUPS = (16, 16, 8, 8)
@@ -51,8 +50,8 @@
 def layer_kernel(
     query, key, value, ids, out,
     meta, slots, qbuf, kbuf, vbuf, hot, qe, ke, weights0, weights1, weights2, weights3,
-    bias0, bias1, split, lq, lk, lv, tails, lout,
-    meta_send, meta_recv, bulk_send, q_recv, k_recv, v_recv, tail_send, tail_recv,
+    bias0, bias1, split, lq, lk, lv, tails, guest, stats, lout,
+    meta_send, meta_recv, bulk_send, q_recv, k_recv, v_recv, tail_send, tail_recv, guest_send, guest_recv,
     load_sem, lout_send, back_send, out_recv, ready,
 ):
     s = lax.axis_index("section")
@@ -75,7 +74,7 @@
                 barrier, inc=1, device_id=(s, (t + j) % PEERS), device_id_type=MESH
             )
 
-    for peer in ((s, prev_t), (prev_s, t), (next_s, t)):
+    for peer in ((s, prev_t), (s, next_t), (prev_s, t), (next_s, t)):
         pl.semaphore_signal(barrier, inc=1, device_id=peer, device_id_type=MESH)
 
     slots[...] = jnp.zeros_like(slots)
@@ -98,7 +97,7 @@
     for load in loads:
         load.start()
 
-    pl.semaphore_wait(barrier, jnp.where(is_owner, HEADS - 1, HEADS) + 3)
+    pl.semaphore_wait(barrier, jnp.where(is_owner, HEADS - 1, HEADS) + 4)
 
     def spread(source, target, send, recv):
         @pl.loop(0, HEADS)
@@ -121,29 +120,34 @@
     def head_block(array):
         return lambda h: array.at[:, pl.ds(pl.multiple_of(HALF + h * HD, HD), HD)]
 
-    def columns(half):
-        return pl.ds(half * EARLY * HD, (EARLY if half == 0 else HEADS - EARLY) * HD)
-
-    def tail_copies(half):
-        return [
-            pltpu.make_async_remote_copy(
-                src_ref=src.at[:, columns(half)], dst_ref=tails.at[a, :, columns(half)],
-                send_sem=tail_send.at[half, a], recv_sem=tail_recv.at[half, a],
-                device_id=(s, next_t), device_id_type=MESH,
-            )
-            for a, src in enumerate((key, value))
-        ]
-
-    def start_tails(half):
-        for copy in tail_copies(half):
+    tail_copies = [
+        pltpu.make_async_remote_copy(
+            src_ref=src.at[:, pl.ds(0, HALF)], dst_ref=tails.at[a],
+            send_sem=tail_send.at[a], recv_sem=tail_recv.at[a],
+            device_id=(s, next_t), device_id_type=MESH,
+        )
+        for a, src in enumerate((key, value))
+    ]
+    visit = pltpu.make_async_remote_copy(
+        src_ref=query.at[:, pl.ds(0, HALF)], dst_ref=guest,
+        send_sem=guest_send.at[0], recv_sem=guest_recv.at[0],
+        device_id=(s, prev_t), device_id_type=MESH,
+    )
+    returns = [
+        pltpu.make_async_remote_copy(
+            src_ref=src, dst_ref=dst, send_sem=guest_send.at[a], recv_sem=guest_recv.at[a],
+            device_id=(s, next_t), device_id_type=MESH,
+        )
+        for a, (src, dst) in enumerate(((guest, tails.at[0]), (stats.at[0], stats.at[1])), 1)
+    ]
+
+    spread(lambda h: slots, meta.at[t], meta_send, meta_recv)
+
+    @pl.when(core == 0)
+    def _():
+        visit.start()
+        for copy in tail_copies:
             copy.start()
-
-    spread(lambda h: slots, meta.at[t], meta_send, meta_recv)
-    start_tails(0)
-
-    @pl.when(core == 0)
-    def _():
-        start_tails(1)
 
     spread(head_block(query), qbuf.at[t], bulk_send.at[0], q_recv.at[z])
     spread(head_block(key), kbuf.at[t], bulk_send.at[1], k_recv.at[z])
@@ -185,31 +189,53 @@
         start = jnp.sum(jnp.where(second, 0.0, 1.0), axis=1, keepdims=True)
         split[...] = by_cluster(jnp.broadcast_to(start, (TOK, TOK)))
 
-    reach = jnp.where(t == 0, TOK, 0)
-    window = cols_at > rows_at + reach
+    window = cols_at > rows_at
     causal = cols_at <= rows_at
-
-    def local_copy(half):
-        return pltpu.make_async_remote_copy(
-            src_ref=lout.at[:, columns(half)], dst_ref=out.at[:, columns(half)],
-            send_sem=lout_send.at[half], recv_sem=out_recv,
-            device_id=(next_s, t), device_id_type=MESH,
-        )
-
-    def local_heads(half):
-        for copy in tail_copies(half):
+    local_copy = pltpu.make_async_remote_copy(
+        src_ref=lout, dst_ref=out.at[:, pl.ds(0, HALF)], send_sem=lout_send, recv_sem=out_recv,
+        device_id=(next_s, t), device_id_type=MESH,
+    )
+
+    def heads_at(g):
+        heads = [g * LOCAL_GROUP + i for i in range(LOCAL_GROUP)]
+        return [(h, pl.ds(pl.multiple_of(h * HD, HD), HD)) for h in heads]
+
+    def soft(scores, mask):
+        scores = jnp.where(mask, scores * SCALE, LOW)
+        top = jnp.max(scores, axis=1, keepdims=True)
+        weights = jnp.exp2(scores - top)
+        return weights.astype(BF16), top, jnp.sum(weights, axis=1, keepdims=True)
+
+    for load in loads:
+        load.wait()
+
+    @pl.when(core == 1)
+    def _():
+        visit.wait_recv()
+
+        def host(g, noted):
+            group = heads_at(g)
+            scores = [dot(guest[:, at], lk[:, at], ((1,), (1,))) for _, at in group]
+            parts = [soft(score, window) for score in scores]
+            mixed = [dot(part[0], lv[:, at]) / part[2] for part, (_, at) in zip(parts, group)]
+            for (h, at), (_, top, total), mix in zip(group, parts, mixed):
+                guest[:, at] = mix.astype(BF16)
+                noted = jnp.where(cols_at == h, top, noted)
+                noted = jnp.where(cols_at == TOK // 2 + h, total, noted)
+            return noted
+
+        stats[0] = lax.fori_loop(0, HEADS // LOCAL_GROUP, host, jnp.zeros((TOK, TOK), F32))
+        for copy in returns:
+            copy.start()
+        for copy in tail_copies:
             copy.wait_recv()
-        lo, hi = (0, EARLY) if half == 0 else (EARLY, HEADS)
-
-        @pl.loop(lo // LOCAL_GROUP, hi // LOCAL_GROUP)
+
+        @pl.loop(0, HEADS // LOCAL_GROUP)
         def _(g):
-            ats = [
-                pl.ds(pl.multiple_of((g * LOCAL_GROUP + i) * HD, HD), HD)
-                for i in range(LOCAL_GROUP)
-            ]
+            group = heads_at(g)
             scores = [
                 (dot(lq[:, at], tails[0, :, at], ((1,), (1,))), dot(lq[:, at], lk[:, at], ((1,), (1,))))
-                for at in ats
+                for _, at in group
             ]
             parts = []
             for before, own in scores:
@@ -221,27 +247,42 @@
                 parts.append((before.astype(BF16), own.astype(BF16), total))
             mixed = [
                 (dot(before, tails[1, :, at]) + dot(own, lv[:, at])) / total
-                for at, (before, own, total) in zip(ats, parts)
+                for (_, at), (before, own, total) in zip(group, parts)
             ]
-            for at, mix in zip(ats, mixed):
+            for (_, at), mix in zip(group, mixed):
                 lout[:, at] = mix.astype(BF16)
 
-        local_copy(half).start()
-
-    for load in loads:
-        load.wait()
-    local_heads(0)
-
-    @pl.when(core == 1)
-    def _():
-        local_heads(1)
+        local_copy.start()
 
     await_sends(bulk_send.at[0], vbuf)
-    @pl.when(core == 1)
-    def _():
-        start_tails(1)
     spread(head_block(value), vbuf.at[t], bulk_send.at[2], v_recv.at[z])
 
+
+    @pl.when(core == 0)
+    def _():
+        for copy in returns:
+            copy.wait_recv()
+        noted = stats[1]
+
+        @pl.loop(0, HEADS // LOCAL_GROUP)
+        def _(g):
+            group = heads_at(g)
+            scores = [dot(lq[:, at], lk[:, at], ((1,), (1,))) for _, at in group]
+            parts = [soft(score, causal) for score in scores]
+            mixed = [dot(part[0], lv[:, at]) for part, (_, at) in zip(parts, group)]
+            for (h, at), (_, top, total), mix in zip(group, parts, mixed):
+                before_top = jnp.sum(jnp.where(cols_at == h, noted, 0.0), axis=1, keepdims=True)
+                before_top = jnp.where(t == 0, LOW, before_top)
+                before_total = jnp.sum(
+                    jnp.where(cols_at == TOK // 2 + h, noted, 0.0), axis=1, keepdims=True
+                )
+                highest = jnp.maximum(top, before_top)
+                before = jnp.exp2(before_top - highest) * before_total
+                own = jnp.exp2(top - highest)
+                both = before * tails[0, :, at].astype(F32) + own * mix
+                lout[:, at] = (both / (before + own * total)).astype(BF16)
+
+        local_copy.start()
 
     @pl.when(is_owner)
     def _():
@@ -338,14 +379,19 @@
 
         pltpu.make_async_copy(vbuf, vbuf, back_send).wait()
 
+    local_copy.wait_send()
+
     @pl.when(core == 0)
     def _():
-        local_heads(1)
-
-    for half in range(2):
-        local_copy(half).wait_send()
-        for copy in tail_copies(half):
+        visit.wait_send()
+        for copy in tail_copies:
             copy.wait_send()
+
+    @pl.when(core == 1)
+    def _():
+        for copy in returns:
+            copy.wait_send()
+
     await_sends(meta_send, meta)
     await_sends(bulk_send.at[1], vbuf)
     await_sends(bulk_send.at[2], vbuf)
@@ -378,8 +424,10 @@
             wide, wide, wide,
             vmem((2, TOK, HALF), BF16),
             wide,
-            dma, dma, dma((3,)), dma((8,)), dma((8,)), dma((8,)), dma((2, 2)), dma((2, 2)),
-            dma((3,)), dma((2,)), dma, dma, pltpu.SemaphoreType.REGULAR,
+            vmem((2, TOK, TOK), F32),
+            wide,
+            dma, dma, dma((3,)), dma((8,)), dma((8,)), dma((8,)), dma((2,)), dma((2,)), dma((3,)), dma((3,)),
+            dma((3,)), dma, dma, dma, pltpu.SemaphoreType.REGULAR,
         ],
         compiler_params=pltpu.CompilerParams(
             collective_id=0, has_side_effects=True, vmem_limit_bytes=60 << 20

time: 109 us -> 106 us (0.972)
  Pallas kernels: 106 us -> 103 us
    pallas_call x1, Pallas kernels: 106 us -> 103 us  [on_device(): pl.pallas_call(layer_kernel, out_shape=jax.ShapeDtypeStruct((TOK, 2 * HAL...]
where the time goes in v4:
time: 106 us
  Pallas kernels  103 us (97%)
  local copies, waits for them, and re-layouts  2.46 us (2%)
    pallas_call x1, Pallas kernels, on_device(): pl.pallas_call(layer_kernel, out_shape=jax.ShapeDtypeStruct((TOK, 2 * HAL...  103 us
    unnamed x1, local copies, waits for them, and re-layouts  2.46 us

profile of v4, /device:TPU:25, one launch (start us, length us, event | category | flops | bytes accessed | tf_op | source)
XLA Modules:
  0.0 105.8 jit_solution(17629884486603858939)
XLA Ops:
  0.0 103.3 %shard_map.46 = bf16[128,5120]{1,0:T(8,128)(2,1)} custom-call(bf16[128,5120]{1,0:T(8,128)(2,1)} %bitcast.8, bf16[128,5120]{1,0:T(8,128)(2,1)} %bitcast.9, bf16[128,5120]{1,0:T(8,128)(2,1)} %bitcast.10, s32[2,128]{1,0:T(2,128)} %bitcast.11), custom_call_target="tpu_custom_call" | custom-call | tf_op jit(solution)/shard_map/pallas_call | solution.py:407
  103.4 2.5 %copy.6 = bf16[1,128,5120]{2,1,0:T(8,128)(2,1)} copy(bf16[1,128,5120]{2,1,0:T(8,128)(2,1)} %bitcast.7) | data formatting | bytes 2621440

commit v5 on v4

--- a/solution.py
+++ b/solution.py
@@ -254,7 +254,6 @@
 
         local_copy.start()
 
-    await_sends(bulk_send.at[0], vbuf)
     spread(head_block(value), vbuf.at[t], bulk_send.at[2], v_recv.at[z])
 
 
@@ -393,6 +392,7 @@
             copy.wait_send()
 
     await_sends(meta_send, meta)
+    await_sends(bulk_send.at[0], vbuf)
     await_sends(bulk_send.at[1], vbuf)
     await_sends(bulk_send.at[2], vbuf)
     pltpu.make_async_copy(out, out, out_recv).wait()

time: 106 us -> 106 us (level)
  no operation moved by 1% of the time
where the time goes in v5:
time: 106 us
  Pallas kernels  103 us (97%)
  local copies, waits for them, and re-layouts  2.46 us (2%)
    pallas_call x1, Pallas kernels, on_device(): pl.pallas_call(layer_kernel, out_shape=jax.ShapeDtypeStruct((TOK, 2 * HAL...  103 us
    unnamed x1, local copies, waits for them, and re-layouts  2.46 us

profile of v5, /device:TPU:25, one launch (start us, length us, event | category | flops | bytes accessed | tf_op | source)
XLA Modules:
  0.0 105.8 jit_solution(4953891129300622840)
XLA Ops:
  0.0 103.3 %shard_map.46 = bf16[128,5120]{1,0:T(8,128)(2,1)} custom-call(bf16[128,5120]{1,0:T(8,128)(2,1)} %bitcast.8, bf16[128,5120]{1,0:T(8,128)(2,1)} %bitcast.9, bf16[128,5120]{1,0:T(8,128)(2,1)} %bitcast.10, s32[2,128]{1,0:T(2,128)} %bitcast.11), custom_call_target="tpu_custom_call" | custom-call | tf_op jit(solution)/shard_map/pallas_call | solution.py:407
  103.3 2.5 %copy.6 = bf16[1,128,5120]{2,1,0:T(8,128)(2,1)} copy(bf16[1,128,5120]{2,1,0:T(8,128)(2,1)} %bitcast.7) | data formatting | bytes 2621440
